TPU v7x, 512 devices: a whole 4x4x16 slice. The times are simulated.
512 devices in a mesh: tm: 16 (over z), height: 8 (over y, core), width: 4 (over x).
Axes of the slice: x: 4, y: 4, z: 16, core: 2. Of those that a mesh axis runs over, the one named last changes fastest.
Arguments:
- video: bfloat16 [3, 64, 256, 1024], P(None, 'tm', 'height', 'width'), may hold values from -6 to 6
- w_conv: bfloat16 [3, 3, 3, 24, 128], replicated, may hold values from -0.25 to 0.25
- w_merge: bfloat16 [512, 512], replicated, may hold values from -0.25 to 0.25
- w_qkv: bfloat16 [512, 1536], replicated, may hold values from -0.25 to 0.25
- w_out: bfloat16 [512, 512], replicated, may hold values from -0.25 to 0.25
Outputs:
- encoded: bfloat16 [32, 64, 256, 512], P('tm', 'height', 'width')
All inputs are finite; a program needn't handle non-finite values.
Results may differ from a plain program's by a relative error of at most 0.013.
Values may be sent and summed in bfloat16 or wider, within the bound.
A program may use at most 192 MiB of HBM per device.

v0:
```python
import math

import jax
import jax.numpy as jnp
from jax import lax
from jax.sharding import PartitionSpec as P

HEADS = 8


def shifted(value, axis, steps):
    count = lax.axis_size(axis)
    initial, last = (max(0, -steps), min(count, count - steps))
    return lax.ppermute(value, axis, [(source, source + steps) for source in range(initial, last)])


def padded_2(cells, sides, width):
    for axis, dim in sides:
        count = lax.axis_size(axis)
        ends = count - 1
        head = lax.slice_in_dim(cells, 0, width, axis=dim)
        tail = lax.slice_in_dim(cells, cells.shape[dim] - width, cells.shape[dim], axis=dim)
        cells = jnp.concatenate(
            [
                lax.ppermute(tail, axis, [(i, (i + 1) % count) for i in range(ends)]),
                cells,
                lax.ppermute(head, axis, [((i + 1) % count, i) for i in range(ends)]),
            ],
            axis=dim,
        )
    return cells


def wavelet(video):
    values = video.astype(jnp.float32)
    chans, frames, rows, cols = values.shape
    values = values.reshape(chans, frames // 2, 2, rows // 2, 2, cols // 2, 2)
    first, second = (values[:, :, 0], values[:, :, 1])
    values = jnp.stack([first + second, first - second], axis=1)
    first, second = (values[:, :, :, :, 0], values[:, :, :, :, 1])
    values = jnp.stack([first + second, first - second], axis=2)
    first, second = (values[..., 0], values[..., 1])
    values = jnp.stack([first + second, first - second], axis=3)
    values = values.reshape(chans * 8, frames // 2, rows // 2, cols // 2)
    return (values * (1.0 / math.sqrt(8.0))).astype(jnp.bfloat16)


def convolve(padded, weight, frames, rows, cols):
    windows = []
    for step_t in range(3):
        for step_h in range(3):
            for step_w in range(3):
                window = padded[
                    :, step_t : step_t + frames, step_h : step_h + rows, step_w : step_w + cols
                ]
                windows.append(window.reshape(padded.shape[0], -1))
    columns = jnp.concatenate(windows, axis=0)
    kernel = weight.reshape(-1, weight.shape[-1])
    total = lax.dot_general(
        kernel, columns, (((0,), (0,)), ((), ())), preferred_element_type=jnp.float32
    )
    return jax.nn.silu(total).reshape(-1, frames, rows, cols).astype(jnp.bfloat16)


def to_tokens(features):
    chans, frames, rows, cols = features.shape
    merged = features.reshape(chans, frames, rows // 2, 2, cols // 2, 2)
    merged = merged.transpose(1, 2, 4, 0, 3, 5)
    return merged.reshape(frames, rows // 2, cols // 2, chans * 4)


def project_in(tokens, w_merge):
    width = w_merge.shape[0]
    latent = jnp.dot(tokens.reshape(-1, width), w_merge, preferred_element_type=jnp.float32).astype(
        jnp.bfloat16
    )
    wide = latent.astype(jnp.float32)
    meansq = jnp.mean(wide * wide, axis=-1, keepdims=True)
    normed = (wide * lax.rsqrt(meansq + 1e-06)).astype(jnp.bfloat16)
    return (latent.reshape(tokens.shape), normed.reshape(tokens.shape))


def attend(combined, heads):
    frames, places, triple = combined.shape
    width = triple // 3
    size = width // heads
    query = combined[..., :width].reshape(frames, places, heads, size).astype(jnp.float32)
    keys = combined[..., width : 2 * width].reshape(frames, places, heads, size).astype(jnp.float32)
    values = combined[..., 2 * width :].reshape(frames, places, heads, size).astype(jnp.float32)
    scores = jnp.einsum("tphd,sphd->phts", query, keys) * size ** (-0.5)
    allowed = jnp.arange(frames)[:, None] >= jnp.arange(frames)[None, :]
    scores = jnp.where(allowed, scores, jnp.float32(-1e30))
    top = jnp.max(scores, axis=-1, keepdims=True)
    expon = jnp.exp(scores - top)
    probs = (expon / jnp.sum(expon, axis=-1, keepdims=True)).astype(jnp.bfloat16)
    mixed = jnp.einsum("phts,sphd->tphd", probs.astype(jnp.float32), values)
    return mixed.reshape(frames, places, width).astype(jnp.bfloat16)


def finish(latent, mixed, w_out):
    width = w_out.shape[0]
    branch = jnp.dot(mixed.reshape(-1, width), w_out, preferred_element_type=jnp.float32)
    total = latent.reshape(-1, width).astype(jnp.float32) + branch
    return total.reshape(latent.shape).astype(jnp.bfloat16)


def shards(video, w_conv, w_merge, w_qkv, w_out):
    bands = wavelet(video)
    subs, frames, rows, cols = bands.shape
    earlier = shifted(bands, "tm", 1)
    joined = jnp.concatenate([earlier, bands], axis=1)
    padded = padded_2(joined, (("height", 2), ("width", 3)), 1)
    features = convolve(padded, w_conv, frames, rows, cols)
    width = w_merge.shape[0]
    tokens = to_tokens(features)
    grid_shape = tokens.shape
    tokens = tokens.reshape(frames, -1, width)
    latent, normed = project_in(tokens, w_merge)
    combined = jnp.dot(normed.reshape(-1, width), w_qkv, preferred_element_type=jnp.float32).astype(
        jnp.bfloat16
    )
    combined = combined.reshape(frames, -1, 3 * width)
    arrived = lax.all_to_all(combined, "tm", split_axis=1, concat_axis=0, tiled=True)
    mixed = attend(arrived, HEADS)
    returned = lax.all_to_all(mixed, "tm", split_axis=0, concat_axis=1, tiled=True)
    return finish(latent, returned, w_out).reshape(grid_shape)


def solution(mesh):
    return jax.shard_map(
        shards,
        mesh=mesh,
        in_specs=(P(None, "tm", "height", "width"), P(), P(), P(), P()),
        out_specs=P("tm", "height", "width", None),
        check_vma=False,
    )
```

profile of v0, /device:TPU:20, one launch (start us, length us, event | category | flops | bytes accessed | tf_op | source)
XLA Modules:
  0.0 462.3 jit_solution(14579761289220698512)
XLA Ops:
  0.0 27.2 %reshape.275 = f32[3,2,2,16,2,128,2]{6,5,4,3,2,1,0:T(8,128)} reshape(bf16[3,4,32,256]{3,2,1,0:T(8,128)(2,1)} %param.5) | data formatting | bytes 589824 | tf_op jit(solution)/shard_map/reshape | solution.py:37
  27.2 14.7 %fusion.5 = f32[3,1,2,16,2,128,2]{6,5,4,3,2,0,1:T(8,128)} fusion(f32[3,2,2,16,2,128,2]{6,5,4,3,2,1,0:T(8,128)} %reshape.275), kind=kLoop, calls=%fused_computation.12 | loop fusion | flops 49152 | bytes 589824 | tf_op jit(solution)/shard_map/add | solution.py:39
  41.9 5.2 %copy-done.1 = f32[3,2,2,16,2,128,2]{6,5,4,3,2,1,0:T(8,128)S(1)} copy-done((f32[3,2,2,16,2,128,2]{6,5,4,3,2,1,0:T(8,128)S(1)}, f32[3,2,2,16,2,128,2]{6,5,4,3,2,1,0:T(8,128)}, u32[]{:S(2)}) %copy-start.1) | copy-done | bytes 393240
  47.1 5.5 %subtract_bitcast_fusion.1 = f32[3,1,2,16,2,128,2]{6,5,4,3,2,0,1:T(8,128)} fusion(f32[3,2,2,16,2,128,2]{6,5,4,3,2,1,0:T(8,128)S(1)} %copy-done.1), kind=kLoop, calls=%fused_computation.14 | loop fusion | flops 49152 | bytes 589824 | tf_op jit(solution)/shard_map/sub | solution.py:39
  52.6 15.7 %fusion.4 = f32[3,2,1,2,16,128,2]{6,5,4,3,0,1,2:T(8,128)} fusion(f32[3,1,2,16,2,128,2]{6,5,4,3,2,0,1:T(8,128)} %subtract_bitcast_fusion.1, f32[3,1,2,16,2,128,2]{6,5,4,3,2,0,1:T(8,128)} %fusion.5), kind=kLoop, calls=%fused_computation.10 | loop fusion | flops 147456 | bytes 589824 | tf_op jit(solution)/shard_map/add | solution.py:41
  68.3 4.2 copy-done.3
  72.5 5.7 %subtract_bitcast_fusion = f32[3,2,1,2,16,128,2]{6,5,4,3,0,1,2:T(8,128)} fusion(f32[3,1,2,16,2,128,2]{6,5,4,3,2,0,1:T(8,128)S(1)} %copy-done.3, f32[3,1,2,16,2,128,2]{6,5,4,3,2,0,1:T(8,128)S(1)} %copy-done.2), kind=kLoop, calls=%fused_computation.13 | loop fusion | flops 147456 | bytes 589824 | tf_op jit(solution)/shard_map/sub | solution.py:41
  78.2 44.0 %fusion.1 = (f32[3,2,2,2,16,128,1]{6,5,4,3,0,1,2:T(8,128)}, f32[3,2,2,2,16,128,1]{6,5,4,3,0,1,2:T(8,128)}) fusion(f32[3,2,1,2,16,128,2]{6,5,4,3,0,1,2:T(8,128)} %subtract_bitcast_fusion, f32[3,2,1,2,16,128,2]{6,5,4,3,0,1,2:T(8,128)} %fusion.4), kind=kLoop, calls=%fused_computation.5 | loop fusion | flops 245760 | bytes 786432 | tf_op jit(solution)/shard_map/add | solution.py:43
  122.2 14.7 %copy.100 = f32[3,2,2,2,16,128,1]{5,4,3,2,1,0,6:T(8,128)S(1)} copy(f32[3,2,2,2,16,128,1]{6,5,4,3,0,1,2:T(8,128)} %get-tuple-element.5) | data formatting | bytes 393216 | tf_op jit(solution)/shard_map/add | solution.py:43
  136.9 14.7 %copy.101 = f32[3,2,2,2,16,128,1]{5,4,3,2,1,0,6:T(8,128)S(1)} copy(f32[3,2,2,2,16,128,1]{6,5,4,3,0,1,2:T(8,128)} %get-tuple-element.6) | data formatting | bytes 393216 | tf_op jit(solution)/shard_map/sub | solution.py:43
  151.7 3.8 collective-permute-start
  155.6 0.8 convert_element_type.56
  156.3 3.4 collective-permute-done
  159.7 0.1 pad_maximum_fusion.7
  159.8 1.9 collective-permute-start.1
  161.7 3.6 collective-permute-start.2
  165.4 0.7 pad_maximum_fusion.5
  166.1 1.0 collective-permute-done.2
  167.1 0.3 pad_maximum_fusion.3
  167.4 0.2 fusion.31
  167.7 1.3 copy.103
  168.9 3.1 collective-permute-start.3
  172.0 0.7 copy.105
  172.7 13.7 %collective-permute-start.4 = (bf16[24,4,18,1]{0,1,3,2:T(4,128)(2,1)S(1)}, bf16[24,4,18,1]{0,1,3,2:T(4,128)(2,1)}, u32[]{:S(2)}, u32[]{:S(2)}) collective-permute-start(bf16[24,4,18,1]{0,1,3,2:T(4,128)(2,1)S(1)} %copy.105), channel_id=1, source_target_pairs={{1,0},{2,1},{3,2},{5,4},{6,5},{7,6},{9,8},{10,9},{11,10},{13,12},{... | collective-permute-start | bytes 10376 | tf_op jit(solution)/shard_map/ppermute | solution.py:27
  186.4 0.4 pad_maximum_fusion.4
  186.9 1.0 fusion.29
  187.9 1.1 copy.104
  188.9 1.8 copy.106
  190.7 2.7 pad_maximum_fusion.2
  193.5 1.2 fusion.27
  194.8 0.1 bitcast_dynamic-update-slice_fusion.25
  194.9 0.1 bitcast_dynamic-update-slice_fusion.23
  195.0 0.1 bitcast_dynamic-update-slice_fusion.22
  195.1 0.1 bitcast_dynamic-update-slice_fusion.21
  195.1 0.1 bitcast_dynamic-update-slice_fusion.20
  195.2 0.1 bitcast_dynamic-update-slice_fusion.19
  195.3 0.1 bitcast_dynamic-update-slice_fusion.18
  195.4 0.1 bitcast_dynamic-update-slice_fusion.16
  195.5 0.1 bitcast_dynamic-update-slice_fusion.15
  195.6 0.1 bitcast_dynamic-update-slice_fusion.14
  195.8 0.1 bitcast_dynamic-update-slice_fusion.12
  195.8 0.1 bitcast_dynamic-update-slice_fusion.11
  196.7 2.2 multiply_convert_fusion
  199.0 3.1 copy.108
  202.0 3.2 reshape_reshape_reshape.3
  205.3 0.8 fusion.7
  206.2 1.9 convolution_convert_fusion
  208.0 4.9 %copy.109 = bf16[2,512,1536]{2,0,1:T(2,128)(2,1)} copy(bf16[2,512,1536]{2,1,0:T(8,128)(2,1)S(1)} %bitcast.178) | data formatting | bytes 6291456 | tf_op jit(solution)/shard_map/reshape | solution.py:122
  212.9 17.0 %all-to-all-start = ((bf16[2,512,1536]{2,0,1:T(2,128)(2,1)}), bf16[2,512,1536]{2,0,1:T(2,128)(2,1)}, u32[]{:S(2)}, u32[]{:S(2)}) async-start(bf16[2,512,1536]{2,0,1:T(2,128)(2,1)} %copy.109), calls=%async_computation | async-start | bytes 6291456 | tf_op jit(solution)/shard_map/all_to_all | solution.py:123
  230.0 139.3 %all-to-all-done = bf16[2,512,1536]{2,0,1:T(2,128)(2,1)} async-done(((bf16[2,512,1536]{2,0,1:T(2,128)(2,1)}), bf16[2,512,1536]{2,0,1:T(2,128)(2,1)}, u32[]{:S(2)}, u32[]{:S(2)}) %all-to-all-start) | async-done | bytes 3145760 | tf_op jit(solution)/shard_map/all_to_all | solution.py:123
  369.3 2.4 copy.110
  371.7 0.3 copy.111
  372.0 1.8 fusion.26
  373.8 3.9 reshape.271
  377.7 3.9 reshape.272
  381.5 2.1 reshape.270
  383.6 4.9 %fusion.12 = f32[32,8,32,32]{2,3,1,0:T(8,128)S(1)} fusion(bf16[32,32,8,64]{3,2,1,0:T(8,128)(2,1)} %reshape.272, bf16[32,32,8,64]{3,2,1,0:T(8,128)(2,1)} %reshape.271), kind=kOutput, calls=%fused_computation.29 | convolution fusion | flops 33554432 | bytes 3145728 | tf_op jit(solution)/shard_map/tphd,sphd->phts/dot_general | solution.py:90
  388.6 1.5 fusion.32
  390.2 1.8 convert_bitcast_fusion
  392.0 2.1 copy.116
  394.1 3.2 convert_element_type.66
  397.3 61.6 %all_to_all.33 = bf16[32,32,512]{2,1,0:T(8,128)(2,1)S(1)} all-to-all(bf16[32,32,512]{2,1,0:T(8,128)(2,1)S(1)} %convert_element_type.66), channel_id=1, replica_groups=mesh['tm'=16,'height'=8,'width'=4] {'tm'}, dimensions={0} | all-to-all | bytes 2097152 | tf_op jit(solution)/shard_map/all_to_all | solution.py:125
  458.9 0.1 copy.117
  459.0 2.9 fusion.9
  (54 shorter events, 1.2 us)
Async XLA Ops:
  0.0 206.2 %copy-start = (bf16[512,1536]{1,0:T(8,128)(2,1)S(1)}, bf16[512,1536]{1,0:T(8,128)(2,1)}, u32[]{:S(2)}) copy-start(bf16[512,1536]{1,0:T(8,128)(2,1)} %param.8) | copy-start | bytes 4718596
  27.2 19.9 %copy-start.1 = (f32[3,2,2,16,2,128,2]{6,5,4,3,2,1,0:T(8,128)S(1)}, f32[3,2,2,16,2,128,2]{6,5,4,3,2,1,0:T(8,128)}, u32[]{:S(2)}) copy-start(f32[3,2,2,16,2,128,2]{6,5,4,3,2,1,0:T(8,128)} %reshape.275) | copy-start | bytes 1179652
  52.6 15.7 %copy-start.2 = (f32[3,1,2,16,2,128,2]{6,5,4,3,2,0,1:T(8,128)S(1)}, f32[3,1,2,16,2,128,2]{6,5,4,3,2,0,1:T(8,128)}, u32[]{:S(2)}) copy-start(f32[3,1,2,16,2,128,2]{6,5,4,3,2,0,1:T(8,128)} %fusion.5) | copy-start | bytes 589828
  52.6 20.0 %copy-start.3 = (f32[3,1,2,16,2,128,2]{6,5,4,3,2,0,1:T(8,128)S(1)}, f32[3,1,2,16,2,128,2]{6,5,4,3,2,0,1:T(8,128)}, u32[]{:S(2)}) copy-start(f32[3,1,2,16,2,128,2]{6,5,4,3,2,0,1:T(8,128)} %subtract_bitcast_fusion.1) | copy-start | bytes 589828
  151.7 8.0 %collective-permute-start = (bf16[24,2,16,128]{3,2,1,0:T(8,128)(2,1)S(1)}, bf16[24,2,16,128]{3,2,1,0:T(8,128)(2,1)S(1)}, u32[]{:S(2)}, u32[]{:S(2)}) collective-permute-start(bf16[24,2,16,128]{3,2,1,0:T(8,128)(2,1)S(1)} %bitcast.169), channel_id=1, source_target_pairs={{0,32},{32,64},{64,96},{96,128},{128,160},{160,192},{192,224},{224... | collective-permute-start | bytes 589832 | tf_op jit(solution)/shard_map/ppermute | solution.py:14
  159.8 6.3 %collective-permute-start.1 = (bf16[24,4,1,128]{3,2,1,0:T(2,128)(2,1)S(1)}, bf16[24,4,1,128]{3,2,1,0:T(2,128)(2,1)S(1)}, u32[]{:S(2)}, u32[]{:S(2)}) collective-permute-start(bf16[24,4,1,128]{3,2,1,0:T(2,128)(2,1)S(1)} %get-tuple-element.40), channel_id=1, source_target_pairs={{0,4},{4,8},{8,12},{12,16},{16,20},{20,24},{24,28},{1,5},{5,9},{9,... | collective-permute-start | bytes 73736 | tf_op jit(solution)/shard_map/ppermute | solution.py:25
  161.7 5.4 %collective-permute-start.2 = (bf16[24,4,1,128]{3,2,1,0:T(2,128)(2,1)S(1)}, bf16[24,4,1,128]{3,2,1,0:T(2,128)(2,1)S(1)}, u32[]{:S(2)}, u32[]{:S(2)}) collective-permute-start(bf16[24,4,1,128]{3,2,1,0:T(2,128)(2,1)S(1)} %get-tuple-element.41), channel_id=1, source_target_pairs={{4,0},{8,4},{12,8},{16,12},{20,16},{24,20},{28,24},{5,1},{9,5},{13... | collective-permute-start | bytes 73736 | tf_op jit(solution)/shard_map/ppermute | solution.py:27
  166.1 20.8 %copy-start.11 = (bf16[24,4,1,128]{3,2,1,0:T(2,128)(2,1)}, bf16[24,4,1,128]{3,2,1,0:T(2,128)(2,1)S(1)}, u32[]{:S(2)}) copy-start(bf16[24,4,1,128]{3,2,1,0:T(2,128)(2,1)S(1)} %collective-permute-done.1) | copy-start | bytes 73732
  167.1 19.8 %copy-start.12 = (bf16[24,4,1,128]{3,2,1,0:T(2,128)(2,1)}, bf16[24,4,1,128]{3,2,1,0:T(2,128)(2,1)S(1)}, u32[]{:S(2)}) copy-start(bf16[24,4,1,128]{3,2,1,0:T(2,128)(2,1)S(1)} %collective-permute-done.2) | copy-start | bytes 73732
  168.9 18.9 %collective-permute-start.3 = (bf16[24,4,18,1]{0,1,3,2:T(4,128)(2,1)}, bf16[24,4,18,1]{0,1,3,2:T(4,128)(2,1)S(1)}, u32[]{:S(2)}, u32[]{:S(2)}) collective-permute-start(bf16[24,4,18,1]{0,1,3,2:T(4,128)(2,1)} %copy.103), channel_id=1, source_target_pairs={{0,1},{1,2},{2,3},{4,5},{5,6},{6,7},{8,9},{9,10},{10,11},{12,13},{... | collective-permute-start | bytes 10376 | tf_op jit(solution)/shard_map/ppermute | solution.py:25
  172.7 16.2 %collective-permute-start.4 = (bf16[24,4,18,1]{0,1,3,2:T(4,128)(2,1)S(1)}, bf16[24,4,18,1]{0,1,3,2:T(4,128)(2,1)}, u32[]{:S(2)}, u32[]{:S(2)}) collective-permute-start(bf16[24,4,18,1]{0,1,3,2:T(4,128)(2,1)S(1)} %copy.105), channel_id=1, source_target_pairs={{1,0},{2,1},{3,2},{5,4},{6,5},{7,6},{9,8},{10,9},{11,10},{13,12},{... | collective-permute-start | bytes 10376 | tf_op jit(solution)/shard_map/ppermute | solution.py:27
  190.7 4.1 copy-start.8
  193.5 1.8 copy-start.7
  193.5 2.0 copy-start.6
  193.5 2.3 copy-start.10
  193.5 2.5 copy-start.5
  194.8 1.7 copy-start.9
  194.8 2.0 copy-start.15
  199.0 6.3 %copy-start.13 = (bf16[512,512]{1,0:T(8,128)(2,1)S(1)}, bf16[512,512]{1,0:T(8,128)(2,1)}, u32[]{:S(2)}) copy-start(bf16[512,512]{1,0:T(8,128)(2,1)} %param.7) | copy-start | bytes 1572868
  206.1 1.9 copy-start.16
  212.9 156.4 %all-to-all-start = ((bf16[2,512,1536]{2,0,1:T(2,128)(2,1)}), bf16[2,512,1536]{2,0,1:T(2,128)(2,1)}, u32[]{:S(2)}, u32[]{:S(2)}) async-start(bf16[2,512,1536]{2,0,1:T(2,128)(2,1)} %copy.109), calls=%async_computation | async-start | bytes 6291456 | tf_op jit(solution)/shard_map/all_to_all | solution.py:123
  388.6 1.6 copy-start.4
  392.0 67.0 %copy-start.14 = (bf16[512,512]{1,0:T(8,128)(2,1)S(1)}, bf16[512,512]{1,0:T(8,128)(2,1)}, u32[]{:S(2)}) copy-start(bf16[512,512]{1,0:T(8,128)(2,1)} %param.9) | copy-start | bytes 1572868
where the time goes:
time: 471 us; the launch traced here: 462 us
  waiting for transfers between devices  144 us (31%)
  local copies, waits for them, and re-layouts  107 us (23%)
  other arithmetic  91.5 us (19%)
  blocking collectives  61.6 us (13%)
  starting transfers between devices  43.3 us (9%)
  matrix products  14.6 us (3%)
    all_to_all x1, waiting for transfers between devices, shards(): lax.all_to_all(combined, 'tm', split_axis=1, concat_axis=0, tiled=True)  139 us
    all_to_all x1, blocking collectives, shards(): lax.all_to_all(mixed, 'tm', split_axis=0, concat_axis=1, tiled=True)  61.6 us
    add x1, other arithmetic, wavelet(): values = jnp.stack([first + second, first - second], axis=3)  44 us
    reshape x1, local copies, waits for them, and re-layouts, wavelet(): values = values.reshape(chans, frames // 2, 2, rows // 2, 2, cols // 2, 2)  27.2 us
    ppermute x2, starting transfers between devices, padded_2(): lax.ppermute(head, axis, [((i + 1) % count, i) for i in range(ends)])  17.4 us
    all_to_all x1, starting transfers between devices, shards(): lax.all_to_all(combined, 'tm', split_axis=1, concat_axis=0, tiled=True)  17 us
    add x1, other arithmetic, wavelet(): values = jnp.stack([first + second, first - second], axis=2)  15.7 us
    sub x1, local copies, waits for them, and re-layouts, wavelet(): values = jnp.stack([first + second, first - second], axis=3)  14.7 us
  transfers between devices with their start and end apart: 6, of which 3 were waited for; matrix products, arithmetic and copies ran while one was open for 1% of the time, Pallas kernels for 0%

commit v1 on v0

v1 whole, which is shorter than its diff:
```python
import functools
import math

import jax
import jax.numpy as jnp
from jax import lax
from jax.experimental import pallas as pl
from jax.experimental.pallas import tpu as pltpu
from jax.sharding import PartitionSpec as P

HEADS = 8

CHANS, FRAMES, ROWS, COLS = 3, 4, 32, 256
TIMES = FRAMES // 2
BLOCK = 4
TALL, WIDE = ROWS // BLOCK, COLS // BLOCK
SPAN = 16
ACROSS = WIDE // SPAN
UNIT = 32
STEPS = 80
UNITS = 20
WIDTH = 512
PARTS = 2
LINES = 64
AHEAD = 16
COPIES = 8
DENSE = 96
SPARE = 32
BF16 = jnp.bfloat16
MESH = pl.DeviceIdType.MESH


class Plan:
    def __init__(self, ring):
        self.ring = ring
        self.times = ring * TIMES
        self.blocks = ring // 2
        self.tall = TALL * ACROSS // self.blocks
        self.units = TIMES * (self.tall + 1) // PARTS
        self.tokens = self.times * SPAN
        self.group = self.times * 4
        self.frames = self.times // 2


def index(count):
    return lax.broadcasted_iota(jnp.int32, (count, 1), 0)


def among(value, low, high):
    return (value >= low) & (value < high)


def one_hot(target, width):
    lane = lax.broadcasted_iota(jnp.int32, (target.shape[0], width), 1)
    return jnp.where(lane == target, 1.0, 0.0).astype(BF16)


def strip_rows():
    row = index(128)
    side, rest = row >> 5, row & 31
    target = (rest >> 1) * ROWS + (1 - side) * (ROWS - 2) + (rest & 1)
    used = (rest < 2 * CHANS * FRAMES) & (side < 2)
    return one_hot(jnp.where(used, target, -1), CHANS * FRAMES * ROWS)


def unit_rows():
    row = index(UNITS * UNIT)
    unit, k = row >> 5, row & 31
    late = jnp.where(unit >= TALL + 1, 1, 0)
    plane = (k >> 3) * FRAMES + 2 * late + ((k >> 2) & 1)
    at = (unit - late * (TALL + 1)) * BLOCK + (k & 3) - 2
    used = (unit < 2 * (TALL + 1)) & (k < 24)
    main = jnp.where(used & among(at, 0, ROWS), plane * ROWS + at, -1)
    halo = jnp.where(at < 0, plane * 2 + at + 2, 32 + plane * 2 + at - ROWS)
    halo = jnp.where(used & ~among(at, 0, ROWS), halo, -1)
    return one_hot(main, CHANS * FRAMES * ROWS), one_hot(halo, 128)


def edge_columns():
    row = index(32)
    line = row & 15
    return one_hot(jnp.where(line < 2, line + (1 - (row >> 4)) * (COLS - 2), -1), COLS)


def block_columns():
    row = index(BLOCK * STEPS)
    c = sum(jnp.where(row >= n * STEPS, 1, 0) for n in range(1, BLOCK))
    x = row - c * STEPS
    at = x * BLOCK + c - 2
    main = jnp.where(among(at, 0, COLS), at, -1)
    halo = jnp.where(at < 0, at + 2, jnp.where(x <= WIDE, 16 + at - COLS, -1))
    return one_hot(main, COLS), one_hot(jnp.where(among(at, 0, COLS), -1, halo), 32)


def unit_lanes():
    row = index(512)
    k = row & 31
    target = ((row >> 5) & 3) * 128 + (row >> 7) * 24 + k
    return one_hot(jnp.where(k < 24, target, -1), 512)


def part_rows(plan):
    row = index(LINES)
    late = jnp.where(row >= AHEAD, 1, 0)
    below = row - late * AHEAD
    third = (below * 171) >> 9
    piece = below - 3 * third

    def source(item):
        unit = (item * 3856) >> 16
        return unit * 32 + item - unit * (SPAN + 1)

    width = plan.units * 32
    every = [one_hot(source(row + 5 * late), width)]
    used = (late == 1) | (below < 15)
    for n in range(3):
        item = jnp.where(late == 1, 69, 16) + third
        every.append(one_hot(jnp.where(used & (piece == n), source(item), -1), width))
    return jnp.concatenate(every, axis=0)


def spare_lanes():
    lane = index(128)
    every = [one_hot(jnp.where(lane < DENSE, lane, -1), 128)]
    for piece in range(3):
        at = lane - piece * SPARE
        every.append(one_hot(jnp.where(among(at, 0, SPARE), DENSE + at, -1), 128))
    return jnp.concatenate(every, axis=0)


def part_lanes():
    lane = index(128)
    every = [one_hot(jnp.where(lane < DENSE, lane, -1), 128)]
    for piece in range(3):
        every.append(one_hot(jnp.where(lane >= DENSE, lane - DENSE + piece * SPARE, -1), 128))
    return jnp.concatenate(every, axis=1)


def window_rows(first, units, lines):
    row = index(units * 32)
    item = (first + (row >> 5)) * (SPAN + 1) + (row & 15) + ((row >> 4) & 1)
    main = jnp.where(item < 16, item, jnp.where(among(item, 21, 69), item - 5, -1))
    total = one_hot(main, 4 * lines)
    rest = jnp.where(item < 69, 3 * (item - 16), AHEAD + 3 * (item - 69))
    for piece in range(3):
        at = (1 + piece) * lines + rest + piece
        total += one_hot(jnp.where(main < 0, at, -1), 4 * lines)
    return total


def tap_signs(out_pixel):
    i, j = divmod(out_pixel, 2)
    row = index(512)
    lane = row & 127
    c = sum(jnp.where(lane >= n * 24, 1, 0) for n in range(1, BLOCK))
    k = lane - c * 24
    up, along = ((row >> 8) & 1) * 4 + (k & 3), ((row >> 7) & 1) * 4 + c
    q, r = (up >> 1) - i, (along >> 1) - j
    used = among(q, 0, 3) & among(r, 0, 3) & (lane < DENSE)
    base = jnp.where(used, (q * 3 + r) * 24 + (k >> 3) * 8, 1024)
    odd = ((k >> 2) & 1) * 4 + (up & 1) * 2 + (along & 1)
    band = lax.broadcasted_iota(jnp.int32, (512, 216), 1) - base
    flips = band & odd
    sign = jnp.where(((flips ^ (flips >> 1) ^ (flips >> 2)) & 1) == 1, -1.0, 1.0)
    return jnp.where(among(band, 0, 8), sign, 0.0).astype(BF16)


def merge_order():
    row = index(WIDTH)
    return one_hot((row & 127) * 4 + (row >> 7), WIDTH)


def turned(plan):
    row = index(plan.tokens)
    part = row // plan.group
    rest = row - part * plan.group
    return one_hot((rest >> 2) * SPAN + part * 4 + (rest & 3), plan.tokens)


def turned_back(plan):
    row = index(plan.frames * SPAN)
    target = ((row >> 2) & 3) * (plan.frames * 4) + (row >> 4) * 4 + (row & 3)
    return one_hot(target, plan.frames * SPAN)


def frame_of(plan, start, step):
    return (start + plan.times + step) & (plan.times - 1)


def window_of(plan, start):
    row = index(plan.frames * SPAN)
    return one_hot(frame_of(plan, start, row >> 4) * SPAN + (row & 15), plan.tokens)


def window_turned(plan, start):
    row = index(plan.frames * SPAN)
    part = row // (plan.frames * 4)
    rest = row - part * plan.frames * 4
    frame = frame_of(plan, start, rest >> 2)
    return one_hot(frame * SPAN + part * 4 + (rest & 3), plan.tokens)


def dot(a, b):
    return jnp.dot(a, b, preferred_element_type=jnp.float32)


def dot_t(a, b):
    return lax.dot_general(a, b, (((1,), (1,)), ((), ())), preferred_element_type=jnp.float32)


def kernel(
    plan, counts,
    video_in, w_conv_in, w_merge_in, w_qkv_in, w_out_in,
    out,
    video, w_conv, w_merge, w_qkv, w_out,
    rows_out, rows_in, cols_out, cols_in, corners_out, corners_in,
    parts_out, parts_in,
    patches, taps, merge, latent, normed, queries, pairs, mixed, encoded, turn, back,
    loaded, rows_sent, rows_got, cols_sent, cols_got, corners_sent, corners_got,
    parts_sent, parts_got, out_sent, out_got, own_done,
):
    ring = plan.ring
    me, high, side = lax.axis_index("tm"), lax.axis_index("height"), lax.axis_index("width")
    highs, sides = counts
    above, below = lax.rem(high + highs - 1, highs), lax.rem(high + 1, highs)
    before, after = lax.rem(side + sides - 1, sides), lax.rem(side + 1, sides)

    loads = [
        pltpu.make_async_copy(source, target, loaded.at[n])
        for n, (source, target) in enumerate(
            (
                (video_in, video), (w_conv_in, w_conv), (w_merge_in, w_merge),
                (w_qkv_in, w_qkv), (w_out_in, w_out),
            )
        )
    ]
    loads[0].start()

    barrier = pltpu.get_barrier_semaphore()
    beside = [{"height": peer} for peer in (above, below)]
    beside += [{"width": peer} for peer in (before, after)]
    beside += [{"height": u, "width": v} for u in (above, below) for v in (before, after)]
    for peer in beside:
        pl.semaphore_signal(barrier, inc=1, device_id=peer, device_id_type=MESH)

    def greet(k, _):
        peer = lax.rem(me + k, ring)
        pl.semaphore_signal(barrier, inc=1, device_id={"tm": peer}, device_id_type=MESH)
        return 0

    lax.fori_loop(1, ring, greet, 0)
    for load in loads[1:]:
        load.start()

    strip, edge = strip_rows(), edge_columns()
    unit_main, unit_halo = unit_rows()
    block_main, block_halo = block_columns()
    loads[0].wait()
    pixels = video[...].reshape(CHANS * FRAMES * ROWS, COLS)
    strips = dot(strip, pixels).astype(BF16)
    rows_out[0] = strips[:32]
    rows_out[1] = strips[32:64]
    edges = dot_t(edge, pixels).astype(BF16)
    cols_out[0] = edges[:16]
    cols_out[1] = edges[16:]
    corners = dot_t(edge, strips).astype(BF16)
    corners_out[0] = corners[:16]
    corners_out[1] = corners[16:]
    pl.semaphore_wait(barrier, ring - 1 + len(beside))

    def border_copy(source, target, sent, got, at, into, peer):
        return pltpu.make_async_remote_copy(
            src_ref=source.at[at], dst_ref=target.at[into], send_sem=sent.at[into],
            recv_sem=got.at[into], device_id=peer, device_id_type=MESH,
        )

    border_copies = []
    for down, u in enumerate((below, above)):
        border_copies.append(
            border_copy(rows_out, rows_in, rows_sent, rows_got, down, down, {"height": u})
        )
    for along, v in enumerate((after, before)):
        border_copies.append(
            border_copy(cols_out, cols_in, cols_sent, cols_got, along, along, {"width": v})
        )
    for down, u in enumerate((below, above)):
        for along, v in enumerate((after, before)):
            border_copies.append(
                border_copy(
                    corners_out, corners_in, corners_sent, corners_got, along, down * 2 + along,
                    {"height": u, "width": v},
                )
            )
    for copy in border_copies:
        copy.start()
    inner = dot(unit_main, pixels)
    lanes = unit_lanes()
    place, spare = part_rows(plan), spare_lanes()
    for copy in border_copies:
        copy.wait()

    def kept(value, condition):
        return jnp.where(condition, value, jnp.zeros_like(value))

    has_rows, has_cols = (high > 0, high < highs - 1), (side > 0, side < sides - 1)
    halo = [kept(rows_in[n], has_rows[n]) for n in range(2)]
    halo = jnp.concatenate(halo + [jnp.zeros((64, COLS), BF16)], axis=0)
    units = (inner + dot(unit_halo, halo)).astype(BF16)
    cols = jnp.concatenate([kept(cols_in[n], has_cols[n]) for n in range(2)], axis=0)
    strip_lane = lax.broadcasted_iota(jnp.int32, (16, 128), 1)
    corner = jnp.concatenate(
        [
            jnp.where(
                strip_lane < 32,
                kept(corners_in[n], has_rows[0] & has_cols[n]),
                kept(corners_in[2 + n], has_rows[1] & has_cols[n]),
            )
            for n in range(2)
        ],
        axis=0,
    )
    sidelong = (dot_t(cols, unit_main) + dot_t(corner, unit_halo)).astype(BF16)
    spread = (dot_t(block_main, units) + dot(block_halo, sidelong)).astype(BF16)

    stacked = jnp.concatenate(
        [
            jnp.concatenate(
                [spread[c * STEPS : (c + 1) * STEPS, q * 128 : (q + 1) * 128] for c in range(4)], axis=1
            )
            for q in range(UNITS // 4)
        ],
        axis=0,
    )
    stacked = dot(stacked, lanes).astype(BF16)

    def piece(t, up, jx):
        q, u = divmod(t * (TALL + 1) + up, 4)
        start = q * STEPS + jx * SPAN
        return stacked[start : start + 32, u * 128 : (u + 1) * 128]

    def pack(part):
        every = []
        for block in range(plan.blocks):
            jy, jx = divmod(block, ACROSS)
            pieces = []
            for unit in range(part * plan.units, (part + 1) * plan.units):
                up, t = divmod(unit, TIMES)
                pieces.append(piece(t, jy * plan.tall + up, jx))
            every.append(jnp.concatenate(pieces, axis=0))
        placed = dot(place, jnp.concatenate(every, axis=1)).astype(BF16)
        placed = [
            jnp.concatenate(
                [
                    placed[n * LINES : (n + 1) * LINES, block * 128 : (block + 1) * 128]
                    for n in range(4)
                ],
                axis=1,
            )
            for block in range(plan.blocks)
        ]
        return dot(jnp.concatenate(placed, axis=0), spare).astype(BF16)

    stages = ((0, 0, LINES), (1, 0, AHEAD), (1, AHEAD, LINES - AHEAD))

    def part_copy(stage, source, target):
        part, start, count = stages[stage]
        return pltpu.make_async_remote_copy(
            src_ref=parts_out.at[part, lax.rem(target, plan.blocks), pl.ds(start, count)],
            dst_ref=parts_in.at[part, source, pl.ds(start, count)],
            send_sem=parts_sent.at[stage, target], recv_sem=parts_got.at[stage, source],
            device_id={"tm": target}, device_id_type=MESH,
        )

    def ahead_by(k):
        step = ring - k
        ahead = (step + 1) // 2
        return lax.select(lax.rem(step, 2) == 1, ahead, ring - ahead)

    def send_parts(stage):
        def send(k, _):
            part_copy(stage, me, lax.rem(me + ahead_by(k), ring)).start()
            return 0

        lax.fori_loop(1, ring, send, 0)

    for part in range(PARTS):
        packed = pack(part)
        for block in range(plan.blocks):
            parts_out[part, block] = packed[block * LINES : (block + 1) * LINES]
        for stage in ((0,), (1, 2))[part]:
            send_parts(stage)
        parts_in[part, me] = parts_out[part, lax.rem(me, plan.blocks)]

    loads[1].wait()
    for out_pixel in range(4):
        signs = tap_signs(out_pixel)
        for dt in range(3):
            taps[dt * WIDTH : (dt + 1) * WIDTH, out_pixel * 128 : (out_pixel + 1) * 128] = (
                dot(signs, w_conv[dt]) * (1.0 / math.sqrt(8.0))
            ).astype(BF16)
    loads[2].wait()
    merge[...] = dot(merge_order(), w_merge[...]).astype(BF16)
    turn[...] = turned(plan)
    back[...] = turned_back(plan)
    for y in range(plan.tall):
        patches[y, 0 : 2 * SPAN, :] = jnp.zeros((2 * SPAN, WIDTH), BF16)
    loads[3].wait()
    loads[4].wait()

    apart = part_lanes()

    def take(stage):
        part, start, count = stages[stage]
        lines = start + count
        first, units = ((0, plan.units), (0, 1), (1, plan.units - 1))[stage]
        batch = (4, 16, 8)[stage]
        pick = window_rows(first, units, lines)

        def one(k, _):
            sources = []
            for n in range(batch):
                at = k * batch + n + 1
                source = lax.rem(me + ahead_by(at), ring)
                sources.append(source)

                @pl.when(at < ring)
                def _():
                    part_copy(stage, source, me).wait_recv()

            rows = jnp.concatenate([parts_in[part, source, :lines] for source in sources], axis=0)
            rows = dot(rows, apart).astype(BF16)
            rows = jnp.concatenate(
                [
                    jnp.concatenate(
                        [
                            rows[n * lines : (n + 1) * lines, copy * 128 : (copy + 1) * 128]
                            for copy in range(4)
                        ],
                        axis=0,
                    )
                    for n in range(batch)
                ],
                axis=1,
            )
            windows = dot(pick, rows).astype(BF16)
            for n, source in enumerate(sources):
                for unit in range(units):
                    up, t = divmod(part * plan.units + first + unit, TIMES)
                    at = pl.multiple_of((source * TIMES + t + 2) * SPAN, SPAN)
                    for dx in range(2):
                        row = unit * 32 + dx * SPAN
                        value = windows[row : row + SPAN, n * 128 : (n + 1) * 128]
                        for dy in range(2):
                            if 0 <= up - dy < plan.tall:
                                tap = dy * 2 + dx
                                patches[
                                    up - dy, pl.ds(at, SPAN), tap * 128 : (tap + 1) * 128
                                ] = value
            return 0

        lax.fori_loop(0, ring // batch, one, 0)

    half = plan.tokens // 2
    group = plan.group
    lane = lax.broadcasted_iota(jnp.int32, (1, 128), 1)
    head_scale = [
        jnp.where((lane < 64) == (head == 0), 0.125, 0.0).astype(BF16) for head in range(2)
    ]
    ones = jnp.ones((group, 128), BF16)
    some = plan.frames * 4
    query_at = lax.broadcasted_iota(jnp.int32, (2 * some, group), 0) & (some - 1)
    key_at = lax.broadcasted_iota(jnp.int32, (2 * some, group), 1)
    same = (query_at & 3) == (key_at & 3)

    far = ring // 4
    start = (me - far) * TIMES + 1
    queries_turned, window = window_turned(plan, start), window_of(plan, start)
    allowed = same & (frame_of(plan, start, query_at >> 2) >= (key_at >> 2))

    def place_of(source, y, first, count):
        block = lax.rem(source, plan.blocks)
        line = (block // ACROSS) * plan.tall + y
        column = pl.multiple_of(lax.rem(block, ACROSS) * SPAN, SPAN)
        return out.at[pl.ds(first, count), line, pl.ds(column, SPAN), :]

    def out_copies(y, source_of):
        copies = []
        for slot, ahead in enumerate(reach):
            source = source_of(ahead)
            first, count = (0, 1) if ahead == far else (1, 1) if ahead == -far else (0, TIMES)
            at = max(0, (ahead + far) * TIMES - 1)
            copies.append(
                pltpu.make_async_remote_copy(
                    src_ref=encoded.at[y, pl.ds(at, count)],
                    dst_ref=place_of(source, y, first, count),
                    send_sem=out_sent.at[y, slot], recv_sem=out_got.at[y, slot],
                    device_id={"tm": lax.rem(source + ahead + ring, ring)}, device_id_type=MESH,
                )
            )
        return copies

    reach = [way * ahead for ahead in range(far, 0, -1) for way in (1, -1)]

    def own_copy(y):
        return pltpu.make_async_copy(
            encoded.at[y, pl.ds(far * TIMES - 1, TIMES)], place_of(me, y, 0, TIMES), own_done.at[y]
        )

    def one_row(y, _):
        for stage in range(len(stages)):
            pl.when(y == stage)(functools.partial(take, stage))

        for m in range(2):
            at = m * half
            around = [patches[y, at + dt * SPAN : at + dt * SPAN + half, :] for dt in range(3)]
            total = 0.5 * dot(jnp.concatenate(around, axis=1), taps[...])
            active = (total + total * jnp.tanh(total)).astype(BF16)
            value = dot(active, merge[...]).astype(BF16)
            latent[at : at + half, :] = value
            wide = value.astype(jnp.float32)
            meansq = jnp.mean(wide * wide, axis=-1, keepdims=True)
            normed[at : at + half, :] = (wide * lax.rsqrt(meansq + 1e-06)).astype(BF16)

        tokens = dot(queries_turned, normed[...]).astype(BF16)
        queries[...] = dot(tokens, w_qkv[:, :WIDTH]).astype(BF16)
        tokens = dot(turn[...], normed[...]).astype(BF16)
        for part in range(2):
            columns = slice(part * WIDTH, (part + 1) * WIDTH)
            pairs[:, columns] = dot(
                tokens, w_qkv[:, (part + 1) * WIDTH : (part + 2) * WIDTH]
            ).astype(BF16)

        for part in range(SPAN // 4):
            asked = slice(part * some, (part + 1) * some)
            rows = slice(part * group, (part + 1) * group)
            for pair in range(HEADS // 2):
                columns = slice(pair * 128, (pair + 1) * 128)
                query, keys = queries[asked, columns], pairs[rows, columns]
                values = pairs[rows, WIDTH + pair * 128 : WIDTH + (pair + 1) * 128]
                both = jnp.concatenate([query * head_scale[0], query * head_scale[1]], axis=0)
                scores = jnp.where(allowed, dot_t(both, keys), -1e30)
                expon = jnp.exp(scores - jnp.max(scores, axis=-1, keepdims=True)).astype(BF16)
                total = dot(expon, jnp.concatenate([values, ones], axis=1))
                result = total[:, :128] / total[:, 128:]
                mixed[asked, columns] = jnp.where(lane < 64, result[:some], result[some:]).astype(BF16)

        straight = dot(back[...], mixed[...]).astype(BF16)
        total = dot(straight, w_out[...]) + dot(window, latent[...])
        encoded[y] = total.astype(BF16).reshape(plan.frames, SPAN, WIDTH)

        for copy in out_copies(y, lambda ahead: me):
            copy.start()
        own_copy(y).start()
        return 0

    lax.fori_loop(0, plan.tall, one_row, 0)

    def parts_left(k, _):
        for stage in range(len(stages)):
            part_copy(stage, me, lax.rem(me + ahead_by(k), ring)).wait_send()
        return 0

    lax.fori_loop(1, ring, parts_left, 0)

    def all_done(y, _):
        for copy in out_copies(y, lambda ahead: me):
            copy.wait_send()
        for copy in out_copies(y, lambda ahead: lax.rem(me - ahead + ring, ring)):
            copy.wait_recv()
        own_copy(y).wait()
        return 0

    lax.fori_loop(0, plan.tall, all_done, 0)


def copied(value):
    def body(source, target, done):
        rows = value.shape[1]
        copies = []
        for n in range(COPIES):
            at = (n // (COPIES // 2), pl.ds(n % (COPIES // 2) * (rows // (COPIES // 2)), rows // (COPIES // 2)))
            copies.append(pltpu.make_async_copy(source.at[at], target.at[at], done.at[n]))
        for copy in copies:
            copy.start()
        for copy in copies:
            copy.wait()

    return pl.pallas_call(
        body,
        out_shape=jax.ShapeDtypeStruct(value.shape, value.dtype),
        in_specs=[pl.BlockSpec(memory_space=pltpu.VMEM)],
        out_specs=pl.BlockSpec(memory_space=pl.ANY),
        scratch_shapes=[pltpu.SemaphoreType.DMA((COPIES,))],
        compiler_params=pltpu.CompilerParams(vmem_limit_bytes=2**20),
    )(value)


def solution(mesh):
    plan = Plan(mesh.shape["tm"])
    counts = (mesh.shape["height"], mesh.shape["width"])

    def shards(video, w_conv, w_merge, w_qkv, w_out):
        operands = (video, w_conv.reshape(3, 216, 128), w_merge, w_qkv, w_out)
        dma = pltpu.SemaphoreType.DMA
        held = [pltpu.VMEM(one.shape, BF16) for one in operands]
        buffers = [
            (2, 32, COLS), (2, 32, COLS),
            (2, 16, CHANS * FRAMES * ROWS), (2, 16, CHANS * FRAMES * ROWS),
            (2, 16, 128), (4, 16, 128),
            (PARTS, plan.blocks, LINES, 128), (PARTS, plan.ring, LINES, 128),
            (plan.tall, plan.tokens + 2 * SPAN, WIDTH),
            (3 * WIDTH, WIDTH), (WIDTH, WIDTH),
            (plan.tokens, WIDTH), (plan.tokens, WIDTH),
            (plan.frames * SPAN, WIDTH), (plan.tokens, 2 * WIDTH), (plan.frames * SPAN, WIDTH),
            (plan.tall, plan.frames, SPAN, WIDTH),
            (plan.tokens, plan.tokens), (plan.frames * SPAN, plan.frames * SPAN),
        ]
        semaphores = [
            (len(operands),), (2,), (2,), (2,), (2,), (4,), (4,),
            (PARTS + 1, plan.ring), (PARTS + 1, plan.ring),
            (plan.tall, plan.ring // 2), (plan.tall, plan.ring // 2), (plan.tall,),
        ]
        return copied(pl.pallas_call(
            functools.partial(kernel, plan, counts),
            out_shape=pltpu.VMEM((TIMES, TALL, WIDE, WIDTH), BF16),
            in_specs=[pl.BlockSpec(memory_space=pltpu.HBM)] * len(operands),
            out_specs=pl.BlockSpec(memory_space=pl.ANY),
            scratch_shapes=held
            + [pltpu.VMEM(shape, BF16) for shape in buffers]
            + [dma(shape) for shape in semaphores],
            compiler_params=pltpu.CompilerParams(
                collective_id=0, has_side_effects=True, vmem_limit_bytes=56 * 2**20
            ),
            cost_estimate=pl.CostEstimate(
                flops=8 * 10**9, bytes_accessed=6 * 10**6, transcendentals=2 * 10**6
            ),
        )(*operands))

    return jax.shard_map(
        shards,
        mesh=mesh,
        in_specs=(P(None, "tm", "height", "width"), P(), P(), P(), P()),
        out_specs=P("tm", "height", "width", None),
        check_vma=False,
    )
```

time: 471 us -> 72.2 us (0.15)
  the two profiles are of different devices: /device:TPU:20 before, /device:TPU:1 now
where the time goes in v1:
time: 72.2 us; the launch traced here: 72.1 us
  Pallas kernels  72 us (100%)
    pallas_call x1, Pallas kernels, shards(): pl.pallas_call(functools.partial(kernel, plan, counts), out_shape=pltpu.V...  71 us

profile of v1, /device:TPU:1, one launch (start us, length us, event | category | flops | bytes accessed | tf_op | source)
XLA Modules:
  0.0 72.1 jit_solution(881346087066377085)
XLA Ops:
  0.0 71.0 %shard_map.55.source = bf16[2,8,64,512]{3,2,1,0:T(8,128)(2,1)S(1)} custom-call(bf16[3,4,32,256]{3,2,1,0:T(8,128)(2,1)} %video_in.1, bf16[3,216,128]{2,1,0:T(8,128)(2,1)} %bitcast.1, bf16[512,512]{1,0:T(8,128)(2,1)} %w_merge_in.1, bf16[512,1536]{1,0:T(8,128)(2,1)} %w_qkv_in.1, bf16[512,512]{1,0:T(8,128)(2,1)} %w_out_in.1), custom_call_target="tpu_custom_call" | custom-call | flops 8000000000 | bytes 6000000 | tf_op jit(solution)/shard_map/pallas_call | solution.py:623
  71.0 1.0 %shard_map.56 = bf16[2,8,64,512]{3,2,1,0:T(8,128)(2,1)} custom-call(bf16[2,8,64,512]{3,2,1,0:T(8,128)(2,1)S(1)} %shard_map.55.source), custom_call_target="tpu_custom_call" | custom-call | tf_op jit(solution)/shard_map/pallas_call | solution.py:588

commit v2 on v1

--- a/solution.py
+++ b/solution.py
@@ -24,6 +24,7 @@
 LINES = 64
 AHEAD = 16
 COPIES = 8
+EARLY = (5, 6)
 DENSE = 96
 SPARE = 32
 BF16 = jnp.bfloat16
@@ -296,6 +297,76 @@
     inner = dot(unit_main, pixels)
     lanes = unit_lanes()
     place, spare = part_rows(plan), spare_lanes()
+
+    def stack(spread):
+        quads = [
+            jnp.concatenate(
+                [spread[c * STEPS : (c + 1) * STEPS, q * 128 : (q + 1) * 128] for c in range(4)], axis=1
+            )
+            for q in range(spread.shape[1] // 128)
+        ]
+        return dot(jnp.concatenate(quads, axis=0), lanes).astype(BF16)
+
+    def pack(stacked, quads, part, blocks):
+        every = []
+        for block in blocks:
+            jy, jx = divmod(block, ACROSS)
+            pieces = []
+            for unit in range(part * plan.units, (part + 1) * plan.units):
+                up, t = divmod(unit, TIMES)
+                q, u = divmod(t * (TALL + 1) + jy * plan.tall + up, 4)
+                at = quads.index(q) * STEPS + jx * SPAN
+                pieces.append(stacked[at : at + 32, u * 128 : (u + 1) * 128])
+            every.append(jnp.concatenate(pieces, axis=0))
+        placed = dot(place, jnp.concatenate(every, axis=1)).astype(BF16)
+        placed = [
+            jnp.concatenate(
+                [placed[m * LINES : (m + 1) * LINES, n * 128 : (n + 1) * 128] for m in range(4)], axis=1
+            )
+            for n in range(len(blocks))
+        ]
+        packed = dot(jnp.concatenate(placed, axis=0), spare).astype(BF16)
+        for n, block in enumerate(blocks):
+            parts_out[part, block] = packed[n * LINES : (n + 1) * LINES]
+
+    stages = ((0, 0, LINES), (1, 0, AHEAD), (1, AHEAD, LINES - AHEAD))
+
+    def part_copy(stage, source, target):
+        part, start, count = stages[stage]
+        return pltpu.make_async_remote_copy(
+            src_ref=parts_out.at[part, lax.rem(target, plan.blocks), pl.ds(start, count)],
+            dst_ref=parts_in.at[part, source, pl.ds(start, count)],
+            send_sem=parts_sent.at[stage, target], recv_sem=parts_got.at[stage, source],
+            device_id={"tm": target}, device_id_type=MESH,
+        )
+
+    def ahead_by(k):
+        step = ring - k
+        ahead = (step + 1) // 2
+        return lax.select(lax.rem(step, 2) == 1, ahead, ring - ahead)
+
+    def send_parts(stage):
+        def send(k, _):
+            target = lax.rem(me + ahead_by(k), ring)
+
+            @pl.when((stage > 0) | ~among(lax.rem(target, plan.blocks), EARLY[0], EARLY[-1] + 1))
+            def _():
+                part_copy(stage, me, target).start()
+
+            return 0
+
+        lax.fori_loop(1, ring, send, 0)
+
+    quads = (1, 3)
+    early = jnp.concatenate([inner[q * 128 : (q + 1) * 128] for q in quads], axis=0).astype(BF16)
+    pack(stack(dot_t(block_main, early).astype(BF16)), quads, 0, EARLY)
+    for target in range(ring):
+        if target % plan.blocks in EARLY:
+
+            @pl.when(me != target)
+            def _():
+                part_copy(0, me, target).start()
+
     for copy in border_copies:
         copy.wait()
 
@@ -322,74 +393,14 @@
     sidelong = (dot_t(cols, unit_main) + dot_t(corner, unit_halo)).astype(BF16)
     spread = (dot_t(block_main, units) + dot(block_halo, sidelong)).astype(BF16)
 
-    stacked = jnp.concatenate(
-        [
-            jnp.concatenate(
-                [spread[c * STEPS : (c + 1) * STEPS, q * 128 : (q + 1) * 128] for c in range(4)], axis=1
-            )
-            for q in range(UNITS // 4)
-        ],
-        axis=0,
-    )
-    stacked = dot(stacked, lanes).astype(BF16)
-
-    def piece(t, up, jx):
-        q, u = divmod(t * (TALL + 1) + up, 4)
-        start = q * STEPS + jx * SPAN
-        return stacked[start : start + 32, u * 128 : (u + 1) * 128]
-
-    def pack(part):
-        every = []
-        for block in range(plan.blocks):
-            jy, jx = divmod(block, ACROSS)
-            pieces = []
-            for unit in range(part * plan.units, (part + 1) * plan.units):
-                up, t = divmod(unit, TIMES)
-                pieces.append(piece(t, jy * plan.tall + up, jx))
-            every.append(jnp.concatenate(pieces, axis=0))
-        placed = dot(place, jnp.concatenate(every, axis=1)).astype(BF16)
-        placed = [
-            jnp.concatenate(
-                [
-                    placed[n * LINES : (n + 1) * LINES, block * 128 : (block + 1) * 128]
-                    for n in range(4)
-                ],
-                axis=1,
-            )
-            for block in range(plan.blocks)
-        ]
-        return dot(jnp.concatenate(placed, axis=0), spare).astype(BF16)
-
-    stages = ((0, 0, LINES), (1, 0, AHEAD), (1, AHEAD, LINES - AHEAD))
-
-    def part_copy(stage, source, target):
-        part, start, count = stages[stage]
-        return pltpu.make_async_remote_copy(
-            src_ref=parts_out.at[part, lax.rem(target, plan.blocks), pl.ds(start, count)],
-            dst_ref=parts_in.at[part, source, pl.ds(start, count)],
-            send_sem=parts_sent.at[stage, target], recv_sem=parts_got.at[stage, source],
-            device_id={"tm": target}, device_id_type=MESH,
-        )
-
-    def ahead_by(k):
-        step = ring - k
-        ahead = (step + 1) // 2
-        return lax.select(lax.rem(step, 2) == 1, ahead, ring - ahead)
-
-    def send_parts(stage):
-        def send(k, _):
-            part_copy(stage, me, lax.rem(me + ahead_by(k), ring)).start()
-            return 0
-
-        lax.fori_loop(1, ring, send, 0)
-
-    for part in range(PARTS):
-        packed = pack(part)
-        for block in range(plan.blocks):
-            parts_out[part, block] = packed[block * LINES : (block + 1) * LINES]
-        for stage in ((0,), (1, 2))[part]:
-            send_parts(stage)
-        parts_in[part, me] = parts_out[part, lax.rem(me, plan.blocks)]
+    stacked, quads = stack(spread), tuple(range(UNITS // 4))
+    pack(stacked, quads, 0, [block for block in range(plan.blocks) if block not in EARLY])
+    send_parts(0)
+    parts_in[0, me] = parts_out[0, lax.rem(me, plan.blocks)]
+    pack(stacked, quads, 1, range(plan.blocks))
+    send_parts(1)
+    send_parts(2)
+    parts_in[1, me] = parts_out[1, lax.rem(me, plan.blocks)]
 
     loads[1].wait()
     for out_pixel in range(4):
@@ -400,7 +411,7 @@
             ).astype(BF16)
     loads[2].wait()
     merge[...] = dot(merge_order(), w_merge[...]).astype(BF16)
-    turn[...] = turned(plan)
+    turn[: plan.tokens] = turned(plan)
     back[...] = turned_back(plan)
     for y in range(plan.tall):
         patches[y, 0 : 2 * SPAN, :] = jnp.zeros((2 * SPAN, WIDTH), BF16)
@@ -474,7 +485,8 @@
 
     far = ring // 4
     start = (me - far) * TIMES + 1
-    queries_turned, window = window_turned(plan, start), window_of(plan, start)
+    turn[plan.tokens :] = window_turned(plan, start)
+    window = window_of(plan, start)
     allowed = same & (frame_of(plan, start, query_at >> 2) >= (key_at >> 2))
 
     def place_of(source, y, first, count):
@@ -521,9 +533,9 @@
             meansq = jnp.mean(wide * wide, axis=-1, keepdims=True)
             normed[at : at + half, :] = (wide * lax.rsqrt(meansq + 1e-06)).astype(BF16)
 
-        tokens = dot(queries_turned, normed[...]).astype(BF16)
-        queries[...] = dot(tokens, w_qkv[:, :WIDTH]).astype(BF16)
         tokens = dot(turn[...], normed[...]).astype(BF16)
+        queries[...] = dot(tokens[plan.tokens :], w_qkv[:, :WIDTH]).astype(BF16)
+        tokens = tokens[: plan.tokens]
         for part in range(2):
             columns = slice(part * WIDTH, (part + 1) * WIDTH)
             pairs[:, columns] = dot(
@@ -613,7 +625,7 @@
             (plan.tokens, WIDTH), (plan.tokens, WIDTH),
             (plan.frames * SPAN, WIDTH), (plan.tokens, 2 * WIDTH), (plan.frames * SPAN, WIDTH),
             (plan.tall, plan.frames, SPAN, WIDTH),
-            (plan.tokens, plan.tokens), (plan.frames * SPAN, plan.frames * SPAN),
+            (plan.tokens + plan.frames * SPAN, plan.tokens), (plan.frames * SPAN, plan.frames * SPAN),
         ]
         semaphores = [
             (len(operands),), (2,), (2,), (2,), (2,), (4,), (4,),

time: 72.2 us -> 73 us (1.011); the launches traced: 72.1 us -> 71.8 us
  no operation moved by 1% of the time
where the time goes in v2:
time: 73 us; the launch traced here: 71.8 us
  Pallas kernels  71.8 us (98%)
    pallas_call x1, Pallas kernels, shards(): pl.pallas_call(functools.partial(kernel, plan, counts), out_shape=pltpu.V...  70.7 us

profile of v2, /device:TPU:1, one launch (start us, length us, event | category | flops | bytes accessed | tf_op | source)
XLA Modules:
  0.0 71.8 jit_solution(8329450278609020900)
XLA Ops:
  0.0 70.7 %shard_map.55.source = bf16[2,8,64,512]{3,2,1,0:T(8,128)(2,1)S(1)} custom-call(bf16[3,4,32,256]{3,2,1,0:T(8,128)(2,1)} %video_in.1, bf16[3,216,128]{2,1,0:T(8,128)(2,1)} %bitcast.1, bf16[512,512]{1,0:T(8,128)(2,1)} %w_merge_in.1, bf16[512,1536]{1,0:T(8,128)(2,1)} %w_qkv_in.1, bf16[512,512]{1,0:T(8,128)(2,1)} %w_out_in.1), custom_call_target="tpu_custom_call" | custom-call | flops 8000000000 | bytes 6000000 | tf_op jit(solution)/shard_map/pallas_call | solution.py:635
  70.8 1.0 %shard_map.56 = bf16[2,8,64,512]{3,2,1,0:T(8,128)(2,1)} custom-call(bf16[2,8,64,512]{3,2,1,0:T(8,128)(2,1)S(1)} %shard_map.55.source), custom_call_target="tpu_custom_call" | custom-call | tf_op jit(solution)/shard_map/pallas_call | solution.py:600

commit v3 on v1

--- a/solution.py
+++ b/solution.py
@@ -215,7 +215,7 @@
     video, w_conv, w_merge, w_qkv, w_out,
     rows_out, rows_in, cols_out, cols_in, corners_out, corners_in,
     parts_out, parts_in,
-    patches, taps, merge, latent, normed, queries, pairs, mixed, encoded, turn, back,
+    patches, taps, merge, latent, normed, queries, keys, values, mixed, encoded, turn, back, values_weight,
     loaded, rows_sent, rows_got, cols_sent, cols_got, corners_sent, corners_got,
     parts_sent, parts_got, out_sent, out_got, own_done,
 ):
@@ -400,11 +400,12 @@
             ).astype(BF16)
     loads[2].wait()
     merge[...] = dot(merge_order(), w_merge[...]).astype(BF16)
-    turn[...] = turned(plan)
+    turn[: plan.tokens] = turned(plan)
     back[...] = turned_back(plan)
     for y in range(plan.tall):
         patches[y, 0 : 2 * SPAN, :] = jnp.zeros((2 * SPAN, WIDTH), BF16)
     loads[3].wait()
+    values_weight[...] = dot_t(one_hot(index(WIDTH), WIDTH), w_qkv[:, 2 * WIDTH :]).astype(BF16)
     loads[4].wait()
 
     apart = part_lanes()
@@ -466,15 +467,15 @@
     head_scale = [
         jnp.where((lane < 64) == (head == 0), 0.125, 0.0).astype(BF16) for head in range(2)
     ]
-    ones = jnp.ones((group, 128), BF16)
     some = plan.frames * 4
-    query_at = lax.broadcasted_iota(jnp.int32, (2 * some, group), 0) & (some - 1)
-    key_at = lax.broadcasted_iota(jnp.int32, (2 * some, group), 1)
+    query_at = lax.broadcasted_iota(jnp.int32, (group, 2 * some), 1) & (some - 1)
+    key_at = lax.broadcasted_iota(jnp.int32, (group, 2 * some), 0)
     same = (query_at & 3) == (key_at & 3)
 
     far = ring // 4
     start = (me - far) * TIMES + 1
-    queries_turned, window = window_turned(plan, start), window_of(plan, start)
+    turn[plan.tokens :] = window_turned(plan, start)
+    window = window_of(plan, start)
     allowed = same & (frame_of(plan, start, query_at >> 2) >= (key_at >> 2))
 
     def place_of(source, y, first, count):
@@ -521,30 +522,32 @@
             meansq = jnp.mean(wide * wide, axis=-1, keepdims=True)
             normed[at : at + half, :] = (wide * lax.rsqrt(meansq + 1e-06)).astype(BF16)
 
-        tokens = dot(queries_turned, normed[...]).astype(BF16)
-        queries[...] = dot(tokens, w_qkv[:, :WIDTH]).astype(BF16)
         tokens = dot(turn[...], normed[...]).astype(BF16)
-        for part in range(2):
-            columns = slice(part * WIDTH, (part + 1) * WIDTH)
-            pairs[:, columns] = dot(
-                tokens, w_qkv[:, (part + 1) * WIDTH : (part + 2) * WIDTH]
-            ).astype(BF16)
-
-        for part in range(SPAN // 4):
-            asked = slice(part * some, (part + 1) * some)
+        queries[...] = dot(tokens[plan.tokens :], w_qkv[:, :WIDTH]).astype(BF16)
+        tokens = tokens[: plan.tokens]
+        keys[...] = dot(tokens, w_qkv[:, WIDTH : 2 * WIDTH]).astype(BF16)
+        values[...] = dot_t(values_weight[...], tokens).astype(BF16)
+
+        def attended(part, pair):
+            columns = slice(pair * 128, (pair + 1) * 128)
             rows = slice(part * group, (part + 1) * group)
+            query = queries[part * some : (part + 1) * some, columns]
+            both = jnp.concatenate([query * head_scale[0], query * head_scale[1]], axis=0)
+            scores = jnp.where(allowed, dot_t(keys[rows, columns], both), -1e30)
+            expon = jnp.exp(scores - jnp.max(scores, axis=0, keepdims=True))
+            share = 1.0 / jnp.sum(expon, axis=0, keepdims=True)
+            return dot(values[columns, rows], expon.astype(BF16)) * share
+
+        for part in range(0, SPAN // 4, 2):
             for pair in range(HEADS // 2):
-                columns = slice(pair * 128, (pair + 1) * 128)
-                query, keys = queries[asked, columns], pairs[rows, columns]
-                values = pairs[rows, WIDTH + pair * 128 : WIDTH + (pair + 1) * 128]
-                both = jnp.concatenate([query * head_scale[0], query * head_scale[1]], axis=0)
-                scores = jnp.where(allowed, dot_t(both, keys), -1e30)
-                expon = jnp.exp(scores - jnp.max(scores, axis=-1, keepdims=True)).astype(BF16)
-                total = dot(expon, jnp.concatenate([values, ones], axis=1))
-                result = total[:, :128] / total[:, 128:]
-                mixed[asked, columns] = jnp.where(lane < 64, result[:some], result[some:]).astype(BF16)
-
-        straight = dot(back[...], mixed[...]).astype(BF16)
+                left, right = attended(part, pair), attended(part + 1, pair)
+                upper = jnp.where(lane < 64, left[:64], pltpu.roll(right[:64], 64, axis=1))
+                lower = jnp.where(lane < 64, pltpu.roll(left[64:], 64, axis=1), right[64:])
+                mixed[pair * 128 : (pair + 1) * 128, part * some : (part + 2) * some] = (
+                    jnp.concatenate([upper, lower], axis=0).astype(BF16)
+                )
+
+        straight = dot_t(back[...], mixed[...]).astype(BF16)
         total = dot(straight, w_out[...]) + dot(window, latent[...])
         encoded[y] = total.astype(BF16).reshape(plan.frames, SPAN, WIDTH)
 
@@ -611,9 +614,11 @@
             (plan.tall, plan.tokens + 2 * SPAN, WIDTH),
             (3 * WIDTH, WIDTH), (WIDTH, WIDTH),
             (plan.tokens, WIDTH), (plan.tokens, WIDTH),
-            (plan.frames * SPAN, WIDTH), (plan.tokens, 2 * WIDTH), (plan.frames * SPAN, WIDTH),
+            (plan.frames * SPAN, WIDTH), (plan.tokens, WIDTH), (WIDTH, plan.tokens),
+            (WIDTH, plan.frames * SPAN),
             (plan.tall, plan.frames, SPAN, WIDTH),
-            (plan.tokens, plan.tokens), (plan.frames * SPAN, plan.frames * SPAN),
+            (plan.tokens + plan.frames * SPAN, plan.tokens), (plan.frames * SPAN, plan.frames * SPAN),
+            (WIDTH, WIDTH),
         ]
         semaphores = [
             (len(operands),), (2,), (2,), (2,), (2,), (4,), (4,),

time: 72.2 us -> 74.3 us (1.029)
  Pallas kernels: 72 us -> 73.7 us
    pallas_call x1, Pallas kernels: 71 us -> 72.6 us  [shards(): pl.pallas_call(functools.partial(kernel, plan, counts), out_shape=pltpu.V...]
where the time goes in v3:
time: 74.3 us; the launch traced here: 73.7 us
  Pallas kernels  73.7 us (99%)
    pallas_call x1, Pallas kernels, shards(): pl.pallas_call(functools.partial(kernel, plan, counts), out_shape=pltpu.V...  72.6 us

profile of v3, /device:TPU:1, one launch (start us, length us, event | category | flops | bytes accessed | tf_op | source)
XLA Modules:
  0.0 73.7 jit_solution(2316706611379627926)
XLA Ops:
  0.0 72.6 %shard_map.55.source = bf16[2,8,64,512]{3,2,1,0:T(8,128)(2,1)S(1)} custom-call(bf16[3,4,32,256]{3,2,1,0:T(8,128)(2,1)} %video_in.1, bf16[3,216,128]{2,1,0:T(8,128)(2,1)} %bitcast.1, bf16[512,512]{1,0:T(8,128)(2,1)} %w_merge_in.1, bf16[512,1536]{1,0:T(8,128)(2,1)} %w_qkv_in.1, bf16[512,512]{1,0:T(8,128)(2,1)} %w_out_in.1), custom_call_target="tpu_custom_call" | custom-call | flops 8000000000 | bytes 6000000 | tf_op jit(solution)/shard_map/pallas_call | solution.py:628
  72.6 1.0 %shard_map.56 = bf16[2,8,64,512]{3,2,1,0:T(8,128)(2,1)} custom-call(bf16[2,8,64,512]{3,2,1,0:T(8,128)(2,1)S(1)} %shard_map.55.source), custom_call_target="tpu_custom_call" | custom-call | tf_op jit(solution)/shard_map/pallas_call | solution.py:591

commit v4 on v2

--- a/solution.py
+++ b/solution.py
@@ -216,7 +216,7 @@
     video, w_conv, w_merge, w_qkv, w_out,
     rows_out, rows_in, cols_out, cols_in, corners_out, corners_in,
     parts_out, parts_in,
-    patches, taps, merge, latent, normed, queries, pairs, mixed, encoded, turn, back,
+    patches, taps, merge, latent, normed, queries, keys, values, mixed, encoded, turn, back, values_weight,
     loaded, rows_sent, rows_got, cols_sent, cols_got, corners_sent, corners_got,
     parts_sent, parts_got, out_sent, out_got, own_done,
 ):
@@ -416,6 +416,7 @@
     for y in range(plan.tall):
         patches[y, 0 : 2 * SPAN, :] = jnp.zeros((2 * SPAN, WIDTH), BF16)
     loads[3].wait()
+    values_weight[...] = dot_t(one_hot(index(WIDTH), WIDTH), w_qkv[:, 2 * WIDTH :]).astype(BF16)
     loads[4].wait()
 
     apart = part_lanes()
@@ -477,10 +478,9 @@
     head_scale = [
         jnp.where((lane < 64) == (head == 0), 0.125, 0.0).astype(BF16) for head in range(2)
     ]
-    ones = jnp.ones((group, 128), BF16)
     some = plan.frames * 4
-    query_at = lax.broadcasted_iota(jnp.int32, (2 * some, group), 0) & (some - 1)
-    key_at = lax.broadcasted_iota(jnp.int32, (2 * some, group), 1)
+    query_at = lax.broadcasted_iota(jnp.int32, (group, 2 * some), 1) & (some - 1)
+    key_at = lax.broadcasted_iota(jnp.int32, (group, 2 * some), 0)
     same = (query_at & 3) == (key_at & 3)
 
     far = ring // 4
@@ -536,27 +536,29 @@
         tokens = dot(turn[...], normed[...]).astype(BF16)
         queries[...] = dot(tokens[plan.tokens :], w_qkv[:, :WIDTH]).astype(BF16)
         tokens = tokens[: plan.tokens]
-        for part in range(2):
-            columns = slice(part * WIDTH, (part + 1) * WIDTH)
-            pairs[:, columns] = dot(
-                tokens, w_qkv[:, (part + 1) * WIDTH : (part + 2) * WIDTH]
-            ).astype(BF16)
-
-        for part in range(SPAN // 4):
-            asked = slice(part * some, (part + 1) * some)
+        keys[...] = dot(tokens, w_qkv[:, WIDTH : 2 * WIDTH]).astype(BF16)
+        values[...] = dot_t(values_weight[...], tokens).astype(BF16)
+
+        def attended(part, pair):
+            columns = slice(pair * 128, (pair + 1) * 128)
             rows = slice(part * group, (part + 1) * group)
+            query = queries[part * some : (part + 1) * some, columns]
+            both = jnp.concatenate([query * head_scale[0], query * head_scale[1]], axis=0)
+            scores = jnp.where(allowed, dot_t(keys[rows, columns], both), -1e30)
+            expon = jnp.exp(scores - jnp.max(scores, axis=0, keepdims=True))
+            share = 1.0 / jnp.sum(expon, axis=0, keepdims=True)
+            return dot(values[columns, rows], expon.astype(BF16)) * share
+
+        for part in range(0, SPAN // 4, 2):
             for pair in range(HEADS // 2):
-                columns = slice(pair * 128, (pair + 1) * 128)
-                query, keys = queries[asked, columns], pairs[rows, columns]
-                values = pairs[rows, WIDTH + pair * 128 : WIDTH + (pair + 1) * 128]
-                both = jnp.concatenate([query * head_scale[0], query * head_scale[1]], axis=0)
-                scores = jnp.where(allowed, dot_t(both, keys), -1e30)
-                expon = jnp.exp(scores - jnp.max(scores, axis=-1, keepdims=True)).astype(BF16)
-                total = dot(expon, jnp.concatenate([values, ones], axis=1))
-                result = total[:, :128] / total[:, 128:]
-                mixed[asked, columns] = jnp.where(lane < 64, result[:some], result[some:]).astype(BF16)
-
-        straight = dot(back[...], mixed[...]).astype(BF16)
+                left, right = attended(part, pair), attended(part + 1, pair)
+                upper = jnp.where(lane < 64, left[:64], pltpu.roll(right[:64], 64, axis=1))
+                lower = jnp.where(lane < 64, pltpu.roll(left[64:], 64, axis=1), right[64:])
+                mixed[pair * 128 : (pair + 1) * 128, part * some : (part + 2) * some] = (
+                    jnp.concatenate([upper, lower], axis=0).astype(BF16)
+                )
+
+        straight = dot_t(back[...], mixed[...]).astype(BF16)
         total = dot(straight, w_out[...]) + dot(window, latent[...])
         encoded[y] = total.astype(BF16).reshape(plan.frames, SPAN, WIDTH)
 
@@ -623,9 +625,11 @@
             (plan.tall, plan.tokens + 2 * SPAN, WIDTH),
             (3 * WIDTH, WIDTH), (WIDTH, WIDTH),
             (plan.tokens, WIDTH), (plan.tokens, WIDTH),
-            (plan.frames * SPAN, WIDTH), (plan.tokens, 2 * WIDTH), (plan.frames * SPAN, WIDTH),
+            (plan.frames * SPAN, WIDTH), (plan.tokens, WIDTH), (WIDTH, plan.tokens),
+            (WIDTH, plan.frames * SPAN),
             (plan.tall, plan.frames, SPAN, WIDTH),
             (plan.tokens + plan.frames * SPAN, plan.tokens), (plan.frames * SPAN, plan.frames * SPAN),
+            (WIDTH, WIDTH),
         ]
         semaphores = [
             (len(operands),), (2,), (2,), (2,), (2,), (4,), (4,),

time: 73 us -> 78.5 us (1.075)
  the two profiles are of different devices: /device:TPU:1 before, /device:TPU:17 now
where the time goes in v4:
time: 78.5 us; the launch traced here: 78.4 us
  Pallas kernels  78.4 us (100%)
    pallas_call x1, Pallas kernels, shards(): pl.pallas_call(functools.partial(kernel, plan, counts), out_shape=pltpu.V...  77.4 us

profile of v4, /device:TPU:17, one launch (start us, length us, event | category | flops | bytes accessed | tf_op | source)
XLA Modules:
  0.0 78.4 jit_solution(12753194062616312510)
XLA Ops:
  0.0 77.4 %shard_map.55.source = bf16[2,8,64,512]{3,2,1,0:T(8,128)(2,1)S(1)} custom-call(bf16[3,4,32,256]{3,2,1,0:T(8,128)(2,1)} %video_in.1, bf16[3,216,128]{2,1,0:T(8,128)(2,1)} %bitcast.1, bf16[512,512]{1,0:T(8,128)(2,1)} %w_merge_in.1, bf16[512,1536]{1,0:T(8,128)(2,1)} %w_qkv_in.1, bf16[512,512]{1,0:T(8,128)(2,1)} %w_out_in.1), custom_call_target="tpu_custom_call" | custom-call | flops 8000000000 | bytes 6000000 | tf_op jit(solution)/shard_map/pallas_call | solution.py:639
  77.4 1.0 %shard_map.56 = bf16[2,8,64,512]{3,2,1,0:T(8,128)(2,1)} custom-call(bf16[2,8,64,512]{3,2,1,0:T(8,128)(2,1)S(1)} %shard_map.55.source), custom_call_target="tpu_custom_call" | custom-call | tf_op jit(solution)/shard_map/pallas_call | solution.py:602
